TPU v7x, 256 devices: a whole 4x4x8 slice. The times are simulated.
256 devices in a mesh: ctx: 64 (over y, x, z_hi, core), head: 4 (over z_lo).
Axes of the slice: x: 4, y: 4, z: 8 (z_hi: 2, z_lo: 4; z = z_hi * 4 + z_lo), core: 2. Of those that a mesh axis runs over, the one named last changes fastest.
Arguments:
- query: bfloat16 [16384, 5120], P('ctx', 'head'), may hold values from -113 to 113
- key: bfloat16 [16384, 5120], P('ctx', 'head'), may hold values from -6 to 6
- value: bfloat16 [16384, 5120], P('ctx', 'head'), may hold values from -6 to 6
- blocks: int32 [128, 8], P('ctx'), may hold values from 0 to 127, as said below
- counts: int32 [128], P('ctx'), may hold values from 1 to 8, as said below
- buckets: int32 [128, 8, 128, 128], P('ctx', 'head'), may hold values from 0 to 31
- edge: bfloat16 [128, 8, 128, 128], P('ctx', 'head'), may hold values from 0.3984375 to 2.5
- table: float32 [40, 32], replicated, may hold values from -6 to 6
Outputs:
- attended: bfloat16 [16384, 5120], P('ctx', 'head')
Inputs may be any that keep to these rules, and one draw needn't show every extreme that they name: Entry 0 of row g is g itself; the 8 entries of a row are distinct; every entry is a key block on the same context shard of 2 blocks as g or on one of the 3 shards before it, counted cyclically. Only the first counts[g] entries of row g of blocks are live.
All inputs are finite; a program needn't handle non-finite values.
Results may differ from a plain program's by a relative error of at most 0.012.
The roundings to bfloat16 on the way count: a program that leaves them out, or rounds other values in their place, can miss the bound.
Values may be sent and summed in bfloat16 or wider, within the bound.
A program may use at most 64 MiB of HBM per device.

v0:
```python
import jax
import jax.numpy as jnp
from jax import lax
from jax.sharding import PartitionSpec as P

HD = 128
BLK = 128
REACH = 4


def passed_along(value, axis, steps):
    count = lax.axis_size(axis)
    pairs = [(source, (source + steps) % count) for source in range(count)]
    return lax.ppermute(value, axis, pairs)


def lookup_bias(table_rows, bucket_tiles, edge_tiles):
    levels = jnp.arange(table_rows.shape[1], dtype=jnp.int32)
    scaled = jnp.where(
        bucket_tiles[..., None] == levels,
        edge_tiles.astype(jnp.float32)[..., None],
        jnp.float32(0.0),
    )
    looked = jnp.einsum(
        "gnabk,hk->hgnab",
        scaled,
        table_rows,
        precision=lax.Precision.HIGHEST,
        preferred_element_type=jnp.float32,
    )
    return looked.astype(jnp.bfloat16)


def body(query, key, value, blocks, counts, buckets, edge, table):
    rows, width = query.shape
    nheads = width // HD
    qblocks = rows // BLK
    nctx = lax.axis_size("ctx")
    myself = lax.axis_index("ctx")
    scale = HD ** (-0.5)
    tiles = lookup_bias(table, buckets, edge)
    bias = lax.all_to_all(tiles, "head", split_axis=0, concat_axis=2, tiled=True)
    paired = jnp.stack([key, value])
    pieces = [paired]
    current = paired
    for step in range(REACH - 1):
        current = passed_along(current, "ctx", 1)
        pieces.append(current)
    window = jnp.stack(pieces)
    stacked = window.reshape(REACH, 2, qblocks, BLK, width)
    stacked = jnp.transpose(stacked, (0, 2, 1, 3, 4)).reshape(REACH * qblocks, 2, BLK, width)
    home = blocks // qblocks
    behind = (myself - home) % nctx
    slots = behind * qblocks + blocks % qblocks
    queries = query.reshape(qblocks, BLK, nheads, HD)

    def entry(j, carry):
        high, total, accum = carry
        picked = jnp.take(stacked, lax.dynamic_index_in_dim(slots, j, 1, keepdims=False), axis=0)
        keys_now = picked[:, 0].reshape(qblocks, BLK, nheads, HD)
        vals_now = picked[:, 1].reshape(qblocks, BLK, nheads, HD)
        bias_now = lax.dynamic_index_in_dim(bias, j, 2, keepdims=False)
        scores = (
            jnp.einsum("qahd,qbhd->qhab", queries, keys_now, preferred_element_type=jnp.float32)
            * scale
        )
        scores = scores + jnp.transpose(bias_now, (1, 0, 2, 3)).astype(jnp.float32)
        live = (j < counts)[:, None, None, None]
        scores = jnp.where(live, scores, jnp.float32(-1e30))
        new_high = jnp.maximum(high, jnp.max(scores, axis=-1))
        factor = jnp.exp(high - new_high)
        weights = jnp.exp(scores - new_high[..., None]).astype(jnp.bfloat16)
        total = total * factor + jnp.sum(weights.astype(jnp.float32), axis=-1)
        accum = accum * factor[..., None] + jnp.einsum(
            "qhab,qbhd->qhad", weights, vals_now, preferred_element_type=jnp.float32
        )
        return (new_high, total, accum)

    start_high = jnp.full((qblocks, nheads, BLK), -1e30, jnp.float32)
    start_total = jnp.zeros((qblocks, nheads, BLK), jnp.float32)
    start_accum = jnp.zeros((qblocks, nheads, BLK, HD), jnp.float32)
    limit = jnp.max(counts)
    high, total, accum = lax.fori_loop(0, limit, entry, (start_high, start_total, start_accum))
    mixed = accum / total[..., None]
    mixed = jnp.transpose(mixed, (0, 2, 1, 3)).reshape(rows, width)
    return mixed.astype(jnp.bfloat16)


def solution(mesh):
    return jax.shard_map(
        body,
        mesh=mesh,
        in_specs=(
            P("ctx", "head"),
            P("ctx", "head"),
            P("ctx", "head"),
            P("ctx", None),
            P("ctx"),
            P("ctx", "head", None, None),
            P("ctx", "head", None, None),
            P(),
        ),
        out_specs=P("ctx", "head"),
        check_vma=False,
    )
```

profile of v0, /device:TPU:96, one launch (start us, length us, event | category | flops | bytes accessed | tf_op | source)
XLA Modules:
  0.0 332.4 jit_solution(13654939328742125422)
XLA Ops:
  1.0 10.4 %convert_bitcast_fusion.1 = bf16[40,2,2,128,128]{4,0,3,2,1:T(8,128)(2,1)S(1)} fusion(f32[2,2,128,128]{3,2,1,0:T(8,128)S(1)} %convert_element_type.33, s32[2,2,128,128]{3,2,1,0:T(8,128)} %param.15, f32[40,32]{0,1:T(8,128)S(1)} %copy-done), kind=kOutput, calls=%fused_computation.22 | convolution fusion | flops 1013448704 | bytes 5772288 | tf_op jit(solution)/shard_map/gnabk,hk->hgnab/dot_general | solution.py:24
  11.3 3.7 %copy.54 = bf16[40,2,2,128,128]{4,3,2,1,0:T(8,128)(2,1)} copy(bf16[40,2,2,128,128]{4,0,3,2,1:T(8,128)(2,1)S(1)} %convert_bitcast_fusion.1) | data formatting | bytes 10485760 | tf_op jit(solution)/shard_map/convert_element_type | solution.py:31
  15.1 6.1 %all-to-all-start = ((bf16[40,2,2,128,128]{4,3,2,1,0:T(8,128)(2,1)}), bf16[40,2,2,128,128]{4,3,2,1,0:T(8,128)(2,1)}, u32[]{:S(2)}, u32[]{:S(2)}) async-start(bf16[40,2,2,128,128]{4,3,2,1,0:T(8,128)(2,1)} %copy.54), calls=%async_computation | async-start | bytes 10485760 | tf_op jit(solution)/shard_map/all_to_all | solution.py:42
  22.6 149.8 %collective-permute-done = bf16[2,256,1280]{2,1,0:T(8,128)(2,1)S(1)} collective-permute-done((bf16[2,256,1280]{2,1,0:T(8,128)(2,1)S(1)}, bf16[2,256,1280]{2,1,0:T(8,128)(2,1)S(1)}, u32[]{:S(2)}, u32[]{:S(2)}) %collective-permute-start) | collective-permute-done | bytes 1310752 | tf_op jit(solution)/shard_map/ppermute | solution.py:14
  172.4 25.4 %collective-permute-done.1 = bf16[2,256,1280]{2,1,0:T(8,128)(2,1)} collective-permute-done((bf16[2,256,1280]{2,1,0:T(8,128)(2,1)S(1)}, bf16[2,256,1280]{2,1,0:T(8,128)(2,1)}, u32[]{:S(2)}, u32[]{:S(2)}) %collective-permute-start.1) | collective-permute-done | bytes 1310752 | tf_op jit(solution)/shard_map/ppermute | solution.py:14
  199.9 23.4 %collective-permute-done.2 = bf16[2,256,1280]{2,1,0:T(8,128)(2,1)} collective-permute-done((bf16[2,256,1280]{2,1,0:T(8,128)(2,1)}, bf16[2,256,1280]{2,1,0:T(8,128)(2,1)}, u32[]{:S(2)}, u32[]{:S(2)}) %collective-permute-start.2) | collective-permute-done | bytes 1310752 | tf_op jit(solution)/shard_map/ppermute | solution.py:14
  223.3 3.1 pad_maximum_fusion
  226.8 2.7 pad_maximum_fusion.1
  229.5 6.9 %copy.55 = bf16[10,2,4,2,128,128]{5,4,3,2,1,0:T(8,128)(2,1)} copy(bf16[10,2,4,2,128,128]{5,4,3,1,0,2:T(8,128)(2,1)} %bitcast.18) | data formatting | bytes 10485760 | tf_op jit(solution)/shard_map/all_to_all | solution.py:42
  237.7 91.4 %while.14 = (s32[]{:T(128)}, f32[2,10,128]{2,1,0:T(8,128)S(1)}, f32[2,10,128]{2,1,0:T(8,128)S(1)}, f32[2,10,128,128]{3,2,1,0:T(8,128)}, s32[]{:T(128)}, /*index=...) while((s32[]{:T(128)}, f32[2,10,128]{2,1,0:T(8,128)S(1)}, ...), condition=%wide.region_4.5_spmd, body=%wide.region_1.4_spmd.sunk | while | flops 172693520 | bytes 22450396 | solution.py:83
  238.6 3.1 gather_fusion
  243.8 1.7 fusion.34
  246.1 3.1 convolution_add_fusion.2
  249.9 3.1 gather_fusion
  255.1 1.7 fusion.34
  257.4 3.1 convolution_add_fusion.2
  261.2 3.1 gather_fusion
  266.5 1.7 fusion.34
  268.7 3.1 convolution_add_fusion.2
  272.5 3.1 gather_fusion
  277.8 1.7 fusion.34
  280.1 3.1 convolution_add_fusion.2
  283.9 3.1 gather_fusion
  289.1 1.7 fusion.34
  291.4 3.1 convolution_add_fusion.2
  295.2 3.1 gather_fusion
  302.7 3.1 convolution_add_fusion.2
  306.5 3.1 gather_fusion
  314.0 3.1 convolution_add_fusion.2
  317.9 3.1 gather_fusion
  325.4 3.1 convolution_add_fusion.2
  329.1 1.7 fusion.10
  (136 shorter events, 33.8 us)
Async XLA Ops:
  0.0 0.9 copy-start
  15.1 6.1 %copy-start.3 = (bf16[256,1280]{1,0:T(8,128)(2,1)S(1)}, bf16[256,1280]{1,0:T(8,128)(2,1)}, u32[]{:S(2)}) copy-start(bf16[256,1280]{1,0:T(8,128)(2,1)} %param.12) | copy-start | bytes 1966084
  15.1 214.4 %all-to-all-start = ((bf16[40,2,2,128,128]{4,3,2,1,0:T(8,128)(2,1)}), bf16[40,2,2,128,128]{4,3,2,1,0:T(8,128)(2,1)}, u32[]{:S(2)}, u32[]{:S(2)}) async-start(bf16[40,2,2,128,128]{4,3,2,1,0:T(8,128)(2,1)} %copy.54), calls=%async_computation | async-start | bytes 10485760 | tf_op jit(solution)/shard_map/all_to_all | solution.py:42
  21.2 176.6 %copy-start.2 = (bf16[256,1280]{1,0:T(8,128)(2,1)S(1)}, bf16[256,1280]{1,0:T(8,128)(2,1)}, u32[]{:S(2)}) copy-start(bf16[256,1280]{1,0:T(8,128)(2,1)} %param.10) | copy-start | bytes 1966084
  22.5 149.9 %collective-permute-start = (bf16[2,256,1280]{2,1,0:T(8,128)(2,1)S(1)}, bf16[2,256,1280]{2,1,0:T(8,128)(2,1)S(1)}, u32[]{:S(2)}, u32[]{:S(2)}) collective-permute-start(bf16[2,256,1280]{2,1,0:T(8,128)(2,1)S(1)} %get-tuple-element.122), channel_id=1, source_target_pairs={{0,4},{4,8},{8,12},{12,16},{16,20},{20,24},{24,28},{28,32},{32,36}... | collective-permute-start | bytes 3932168 | tf_op jit(solution)/shard_map/ppermute | solution.py:14
  172.4 25.4 %copy-start.1 = (bf16[2,256,1280]{2,1,0:T(8,128)(2,1)}, bf16[2,256,1280]{2,1,0:T(8,128)(2,1)S(1)}, u32[]{:S(2)}) copy-start(bf16[2,256,1280]{2,1,0:T(8,128)(2,1)S(1)} %collective-permute-done) | copy-start | bytes 3932164
  172.4 25.4 %collective-permute-start.1 = (bf16[2,256,1280]{2,1,0:T(8,128)(2,1)S(1)}, bf16[2,256,1280]{2,1,0:T(8,128)(2,1)}, u32[]{:S(2)}, u32[]{:S(2)}) collective-permute-start(bf16[2,256,1280]{2,1,0:T(8,128)(2,1)S(1)} %collective-permute-done), channel_id=1, source_target_pairs={{0,4},{4,8},{8,12},{12,16},{16,20},{20,24},{24,28},{28,32},{32,36}... | collective-permute-start | bytes 3932168 | tf_op jit(solution)/shard_map/ppermute | solution.py:14
  197.7 25.6 %collective-permute-start.2 = (bf16[2,256,1280]{2,1,0:T(8,128)(2,1)}, bf16[2,256,1280]{2,1,0:T(8,128)(2,1)}, u32[]{:S(2)}, u32[]{:S(2)}) collective-permute-start(bf16[2,256,1280]{2,1,0:T(8,128)(2,1)} %collective-permute-done.1), channel_id=1, source_target_pairs={{0,4},{4,8},{8,12},{12,16},{16,20},{20,24},{24,28},{28,32},{32,36}... | collective-permute-start | bytes 3932168 | tf_op jit(solution)/shard_map/ppermute | solution.py:14
  197.7 1.4 copy-start.4
  197.7 1.5 copy-start.5
where the time goes:
time: 334 us; the launch traced here: 332 us
  waiting for transfers between devices  199 us (60%)
  local copies, waits for them, and re-layouts  57.8 us (17%)
  matrix products  49 us (15%)
  other arithmetic  13.9 us (4%)
  loops' own time  6.82 us (2%)
  starting transfers between devices  6.17 us (2%)
    ppermute x3, waiting for transfers between devices, passed_along(): return lax.ppermute(value, axis, pairs)  199 us
    dot_general x8, matrix products, entry(): jnp.einsum('qhab,qbhd->qhad', weights, vals_now, preferred_element_type=j...  25 us
    gather x8, local copies, waits for them, and re-layouts, entry(): jnp.take(stacked, lax.dynamic_index_in_dim(slots, j, 1, keepdims=False),...  24.9 us
    dot_general x8, matrix products, entry(): jnp.einsum('qahd,qbhd->qhab', queries, keys_now, preferred_element_type=j...  13.7 us
    dynamic_slice x16, local copies, waits for them, and re-layouts, entry(): bias_now = lax.dynamic_index_in_dim(bias, j, 2, keepdims=False)  11.8 us
    dot_general x1, matrix products, lookup_bias(): jnp.einsum('gnabk,hk->hgnab', scaled, table_rows, precision=lax.Precision...  10.4 us
    all_to_all x1, local copies, waits for them, and re-layouts, body(): lax.all_to_all(tiles, 'head', split_axis=0, concat_axis=2, tiled=True)  6.94 us
    another operation x1, loops' own time, body(): lax.fori_loop(0, limit, entry, (start_high, start_total, start_accum))  6.82 us
  transfers between devices with their start and end apart: 4, of which 3 were waited for; matrix products, arithmetic and copies ran while one was open for 3% of the time, Pallas kernels for 0%

commit v1 on v0

v1 whole, which is shorter than its diff:
```python
import jax
import jax.numpy as jnp
from jax import lax
from jax.experimental import pallas as pl
from jax.experimental.pallas import tpu as pltpu
from jax.sharding import PartitionSpec as P

HD = 128
BLK = 128
REACH = 4
DEAD = -1e30
MESH = pl.DeviceIdType.MESH


def attention_kernel(
    nctx,
    blocks_ref,
    counts_ref,
    q_hbm,
    k_hbm,
    v_hbm,
    buckets_hbm,
    edge_hbm,
    table_ref,
    out_hbm,
    q_vm,
    kv_own,
    kv_in,
    bucket_raw,
    bucket_all,
    edge_all,
    index_vm,
    edge_vm,
    table_vm,
    scores_vm,
    out_vm,
    local_sem,
    out_sem,
    kv_send,
    kv_recv,
    tile_send,
    tile_recv,
):
    nheads = kv_own.shape[1]
    nlevels = table_ref.shape[1]
    ctx = lax.axis_index("ctx")
    head = lax.axis_index("head")
    core = lax.rem(ctx, 2)
    head_near = head + 1 - 2 * lax.rem(head, 2)
    head_two = lax.rem(head + 2, 4)
    head_far = 3 - head
    middle = jnp.logical_or(head == 1, head == 2)

    def at_ctx(shift):
        return (lax.rem(ctx + shift + nctx, nctx), head)

    next_chip, prev_chip = at_ctx(2), at_ctx(-2)
    third_to, third_from = at_ctx(1 + 2 * core), at_ctx(2 * core - 3)
    partner = at_ctx(1 - 2 * core)

    bucket_load = pltpu.make_async_copy(buckets_hbm, bucket_raw, local_sem.at[0])
    edge_load = pltpu.make_async_copy(edge_hbm, edge_all.at[head], local_sem.at[1])
    q_load = pltpu.make_async_copy(q_hbm, q_vm, local_sem.at[2])
    bucket_load.start()
    edge_load.start()
    q_load.start()

    def own_load(pair, c):
        src = (k_hbm, v_hbm)[pair]
        return pltpu.make_async_copy(
            src.at[:, pl.ds(pl.multiple_of(c * HD, HD), HD)],
            kv_own.at[pair, c],
            local_sem.at[3 + pair * nheads + c],
        )

    def load_own(c, carry):
        own_load(0, c).start()
        own_load(1, c).start()
        return carry

    lax.fori_loop(0, nheads, load_own, 0)

    barrier = pltpu.get_barrier_semaphore()
    peers = [
        next_chip,
        prev_chip,
        third_to,
        third_from,
        (ctx, head_near),
        (ctx, head_two),
        (ctx, head_far),
    ]
    for peer in peers:
        pl.semaphore_signal(barrier, inc=1, device_id=peer, device_id_type=MESH)
    pl.semaphore_wait(barrier, len(peers))

    def kv_copy(flow, pair, c, target):
        if flow == 1:
            src = kv_in.at[0, pair, c]
        else:
            src = (k_hbm, v_hbm)[pair].at[:, pl.ds(pl.multiple_of(c * HD, HD), HD)]
        return pltpu.make_async_remote_copy(
            src_ref=src,
            dst_ref=kv_in.at[flow, pair, c],
            send_sem=kv_send.at[flow, pair, c],
            recv_sem=kv_recv.at[flow, pair, c],
            device_id=target,
            device_id_type=MESH,
        )

    def tile_copy(which, origin, slot, target):
        if which == 0:
            src = bucket_all.at[origin]
            dst = bucket_all.at[origin]
        else:
            src = edge_all.at[origin]
            dst = edge_all.at[origin]
        return pltpu.make_async_remote_copy(
            src_ref=src,
            dst_ref=dst,
            send_sem=tile_send.at[which, slot],
            recv_sem=tile_recv.at[which, origin],
            device_id=(ctx, target),
            device_id_type=MESH,
        )

    bucket_load.wait()
    bucket_all[head] = bucket_raw[...].astype(jnp.float32).astype(jnp.bfloat16)
    edge_load.wait()
    for which in range(2):
        tile_copy(which, head, 1, head_two).start()
        tile_copy(which, head, 0, head_near).start()

    @pl.when(middle)
    def _():
        for which in range(2):
            tile_copy(which, head, 2, head_far).start()

    def send_own(c, carry):
        for pair in range(2):
            kv_copy(0, pair, c, next_chip).start()
        for pair in range(2):
            kv_copy(2, pair, c, third_to).start()
        return carry

    lax.fori_loop(0, nheads, send_own, 0)

    table_vm[...] = jnp.full_like(table_vm, DEAD)
    table_vm[:, 0:nlevels] = table_ref[...]

    for which in range(2):
        tile_copy(which, head_two, 1, head_two).wait_recv()

    @pl.when(middle)
    def _():
        for which in range(2):
            tile_copy(which, head_two, 3, head_near).start()

    for which in range(2):
        tile_copy(which, head_near, 0, head_near).wait_recv()
        tile_copy(which, head_far, 2, head_near).wait_recv()

    behind = (0, 2, 1 + 2 * core, 3 - 2 * core)
    for g in range(2):
        for j in range(REACH):
            home = lax.rem(ctx - behind[j] + nctx, nctx)
            for b in range(2):
                block = home * 2 + b
                entry = jnp.int32(0)
                for n in range(8):
                    entry = jnp.where(blocks_ref[g, n] == block, n, entry)
                dead = entry >= counts_ref[g]
                origin, part = entry // 2, entry % 2
                found = bucket_all[origin, g, part].astype(jnp.float32).astype(jnp.int32)
                index_vm[g, j * 2 + b] = jnp.where(dead, nlevels, found)
                edge_vm[g, j * 2 + b] = edge_all[origin, g, part].astype(jnp.float32)

    q_load.wait()
    scale = HD ** (-0.5)

    def one_head(c, carry):
        for pair in range(2):
            kv_copy(0, pair, c, next_chip).wait_recv()
            kv_copy(1, pair, c, partner).start()
        for pair in range(2):
            own_load(pair, c).wait()
            kv_copy(2, pair, c, third_to).wait_recv()
        for pair in range(2):
            kv_copy(1, pair, c, partner).wait_recv()

        queries = q_vm[:, pl.ds(pl.multiple_of(c * HD, HD), HD)]
        row = table_vm[pl.ds(head * nheads + c, 1), :]
        levels = jnp.broadcast_to(row, (BLK, HD))
        high = [jnp.full((BLK, BLK), -jnp.inf, jnp.float32) for _ in range(2)]
        for j in range(REACH):
            keys = kv_own[0, c] if j == 0 else kv_in[j - 1, 0, c]
            raw = lax.dot_general(
                queries, keys, (((1,), (1,)), ((), ())), preferred_element_type=jnp.float32
            )
            for g in range(2):
                for b in range(2):
                    looked = jnp.take_along_axis(levels, index_vm[g, j * 2 + b], axis=1)
                    bias = (looked * edge_vm[g, j * 2 + b]).astype(jnp.bfloat16)
                    tile = raw[g * BLK : (g + 1) * BLK, b * BLK : (b + 1) * BLK] * scale
                    tile = tile + bias.astype(jnp.float32)
                    high[g] = jnp.maximum(high[g], tile)
                    scores_vm[pl.ds(g * BLK, BLK), pl.ds((j * 2 + b) * BLK, BLK)] = tile
        top = jnp.concatenate([jnp.max(x, axis=1, keepdims=True) for x in high], axis=0)
        mixed = jnp.zeros((2 * BLK, 2 * HD), jnp.float32)
        ones = jnp.ones((2 * BLK, HD), jnp.bfloat16)
        for j in range(REACH):
            vals = kv_own[1, c] if j == 0 else kv_in[j - 1, 1, c]
            weights = jnp.exp(scores_vm[:, pl.ds(j * 2 * BLK, 2 * BLK)] - top)
            mixed = mixed + jnp.dot(
                weights.astype(jnp.bfloat16),
                jnp.concatenate([vals, ones], axis=1),
                preferred_element_type=jnp.float32,
            )
        out_vm[c] = (mixed[:, :HD] / mixed[:, HD:]).astype(jnp.bfloat16)
        out_copy(c).start()
        return carry

    def out_copy(c):
        return pltpu.make_async_copy(
            out_vm.at[c],
            out_hbm.at[:, pl.ds(pl.multiple_of(c * HD, HD), HD)],
            out_sem.at[c],
        )

    lax.fori_loop(0, nheads, one_head, 0)

    def finish(c, carry):
        out_copy(c).wait()
        for pair in range(2):
            kv_copy(0, pair, c, next_chip).wait_send()
            kv_copy(1, pair, c, partner).wait_send()
            kv_copy(2, pair, c, third_to).wait_send()
        return carry

    lax.fori_loop(0, nheads, finish, 0)
    for which in range(2):
        tile_copy(which, head, 1, head_two).wait_send()
        tile_copy(which, head, 0, head_near).wait_send()

    @pl.when(middle)
    def _():
        for which in range(2):
            tile_copy(which, head, 2, head_far).wait_send()
            tile_copy(which, head_two, 3, head_near).wait_send()


def body(query, key, value, blocks, counts, buckets, edge, table):
    rows, width = query.shape
    nheads = width // HD
    nctx = lax.axis_size("ctx")
    anywhere = pl.BlockSpec(memory_space=pl.ANY)
    scalars = pl.BlockSpec(memory_space=pltpu.SMEM)
    tiles = (2, 2, BLK, BLK)

    def kernel(*refs):
        attention_kernel(nctx, *refs)

    return pl.pallas_call(
        kernel,
        out_shape=jax.ShapeDtypeStruct((rows, width), jnp.bfloat16),
        in_specs=[scalars, scalars] + [anywhere] * 5 + [pl.BlockSpec(memory_space=pltpu.VMEM)],
        out_specs=anywhere,
        scratch_shapes=[
            pltpu.VMEM((rows, width), jnp.bfloat16),
            pltpu.VMEM((2, nheads, rows, HD), jnp.bfloat16),
            pltpu.VMEM((3, 2, nheads, rows, HD), jnp.bfloat16),
            pltpu.VMEM(tiles, jnp.int32),
            pltpu.VMEM((4,) + tiles, jnp.bfloat16),
            pltpu.VMEM((4,) + tiles, jnp.bfloat16),
            pltpu.VMEM((2, 8, BLK, BLK), jnp.int32),
            pltpu.VMEM((2, 8, BLK, BLK), jnp.float32),
            pltpu.VMEM((table.shape[0], 128), jnp.float32),
            pltpu.VMEM((rows, 8 * BLK), jnp.float32),
            pltpu.VMEM((nheads, rows, HD), jnp.bfloat16),
            pltpu.SemaphoreType.DMA((3 + 2 * nheads,)),
            pltpu.SemaphoreType.DMA((nheads,)),
            pltpu.SemaphoreType.DMA((3, 2, nheads)),
            pltpu.SemaphoreType.DMA((3, 2, nheads)),
            pltpu.SemaphoreType.DMA((2, 4)),
            pltpu.SemaphoreType.DMA((2, 4)),
        ],
        compiler_params=pltpu.CompilerParams(
            collective_id=0, has_side_effects=True, vmem_limit_bytes=60 * 2**20
        ),
        name="attention",
    )(blocks, counts, query, key, value, buckets, edge, table)


def solution(mesh):
    return jax.shard_map(
        body,
        mesh=mesh,
        in_specs=(
            P("ctx", "head"),
            P("ctx", "head"),
            P("ctx", "head"),
            P("ctx", None),
            P("ctx"),
            P("ctx", "head", None, None),
            P("ctx", "head", None, None),
            P(),
        ),
        out_specs=P("ctx", "head"),
        check_vma=False,
    )
```

time: 334 us -> 119 us (0.36)
  the two profiles are of different devices: /device:TPU:96 before, /device:TPU:32 now
where the time goes in v1:
time: 119 us; the launch traced here: 117 us
  Pallas kernels  114 us (96%)
  local copies, waits for them, and re-layouts  3.37 us (3%)
    pallas_call x1, Pallas kernels, body(): pl.pallas_call(kernel, out_shape=jax.ShapeDtypeStruct((rows, width), jnp....  114 us
    unnamed x2, local copies, waits for them, and re-layouts  3.37 us

profile of v1, /device:TPU:32, one launch (start us, length us, event | category | flops | bytes accessed | tf_op | source)
XLA Modules:
  0.0 117.4 jit_solution(8161150583912703982)
XLA Ops:
  0.0 1.4 %copy.9.refs_7_ = f32[40,32]{1,0:T(8,128)} copy(f32[40,32]{0,1:T(8,128)} %param.15) | data formatting | bytes 10240 | tf_op args[7]
  1.4 114.1 %attention.1 = bf16[256,1280]{1,0:T(8,128)(2,1)} custom-call(s32[2,8]{1,0:T(2,128)} %refs_0_.1, s32[2]{0:T(128)} %refs_1_.1, bf16[256,1280]{1,0:T(8,128)(2,1)} %refs_2_.1, bf16[256,1280]{1,0:T(8,128)(2,1)} %refs_3_.1, bf16[256,1280]{1,0:T(8,128)(2,1)} %refs_4_.1, s32[2,2,128,128]{3,2,1,0:T(8,128)} %refs_5_.1, bf16[2,2,128,128]{3,2,1,0:T(8,128)(2,1)} %refs_6_.1, ...), custom_call_target="tpu_custom_call" | custom-call | tf_op jit(solution)/shard_map/attention/pallas_call | solution.py:263
  115.5 2.0 %copy.11 = bf16[256,1280]{1,0:T(8,128)(2,1)} copy(bf16[256,1280]{1,0:T(8,128)(2,1)} %attention.1) | data formatting | bytes 1310720

commit v2 on v1

--- a/solution.py
+++ b/solution.py
@@ -1,3 +1,5 @@
+import functools
+
 import jax
 import jax.numpy as jnp
 from jax import lax
@@ -9,6 +11,8 @@
 BLK = 128
 REACH = 4
 DEAD = -1e30
+PIECE = 2
+AHEAD = 2
 MESH = pl.DeviceIdType.MESH
 
 
@@ -21,7 +25,7 @@
     v_hbm,
     buckets_hbm,
     edge_hbm,
-    table_ref,
+    table_hbm,
     out_hbm,
     q_vm,
     kv_own,
@@ -31,6 +35,7 @@
     edge_all,
     index_vm,
     edge_vm,
+    table_raw,
     table_vm,
     scores_vm,
     out_vm,
@@ -41,8 +46,10 @@
     tile_send,
     tile_recv,
 ):
-    nheads = kv_own.shape[1]
-    nlevels = table_ref.shape[1]
+    pieces = kv_own.shape[1]
+    nheads = out_vm.shape[0]
+    wide = PIECE * HD
+    nlevels = table_raw.shape[1]
     ctx = lax.axis_index("ctx")
     head = lax.axis_index("head")
     core = lax.rem(ctx, 2)
@@ -61,16 +68,18 @@
     bucket_load = pltpu.make_async_copy(buckets_hbm, bucket_raw, local_sem.at[0])
     edge_load = pltpu.make_async_copy(edge_hbm, edge_all.at[head], local_sem.at[1])
     q_load = pltpu.make_async_copy(q_hbm, q_vm, local_sem.at[2])
+    table_load = pltpu.make_async_copy(table_hbm, table_raw, local_sem.at[3])
     bucket_load.start()
     edge_load.start()
     q_load.start()
+    table_load.start()
 
     def own_load(pair, c):
         src = (k_hbm, v_hbm)[pair]
         return pltpu.make_async_copy(
-            src.at[:, pl.ds(pl.multiple_of(c * HD, HD), HD)],
+            src.at[:, pl.ds(pl.multiple_of(c * wide, HD), wide)],
             kv_own.at[pair, c],
-            local_sem.at[3 + pair * nheads + c],
+            local_sem.at[4 + pair * pieces + c],
         )
 
     def load_own(c, carry):
@@ -78,7 +87,7 @@
         own_load(1, c).start()
         return carry
 
-    lax.fori_loop(0, nheads, load_own, 0)
+    lax.fori_loop(0, pieces, load_own, 0)
 
     barrier = pltpu.get_barrier_semaphore()
     peers = [
@@ -98,7 +107,7 @@
         if flow == 1:
             src = kv_in.at[0, pair, c]
         else:
-            src = (k_hbm, v_hbm)[pair].at[:, pl.ds(pl.multiple_of(c * HD, HD), HD)]
+            src = (k_hbm, v_hbm)[pair].at[:, pl.ds(pl.multiple_of(c * wide, HD), wide)]
         return pltpu.make_async_remote_copy(
             src_ref=src,
             dst_ref=kv_in.at[flow, pair, c],
@@ -143,10 +152,11 @@
             kv_copy(2, pair, c, third_to).start()
         return carry
 
-    lax.fori_loop(0, nheads, send_own, 0)
-
+    lax.fori_loop(0, AHEAD, send_own, 0)
+
+    table_load.wait()
     table_vm[...] = jnp.full_like(table_vm, DEAD)
-    table_vm[:, 0:nlevels] = table_ref[...]
+    table_vm[:, 0:nlevels] = table_raw[...]
 
     for which in range(2):
         tile_copy(which, head_two, 1, head_two).wait_recv()
@@ -178,22 +188,31 @@
     q_load.wait()
     scale = HD ** (-0.5)
 
-    def one_head(c, carry):
+    def one_piece(c, carry):
         for pair in range(2):
             kv_copy(0, pair, c, next_chip).wait_recv()
             kv_copy(1, pair, c, partner).start()
+
+        @pl.when(c + AHEAD < pieces)
+        def _():
+            send_own(c + AHEAD, 0)
+
         for pair in range(2):
             own_load(pair, c).wait()
             kv_copy(2, pair, c, third_to).wait_recv()
         for pair in range(2):
             kv_copy(1, pair, c, partner).wait_recv()
-
+        return lax.fori_loop(0, PIECE, functools.partial(one_head, c), carry)
+
+    def one_head(piece, part, carry):
+        c = piece * PIECE + part
+        columns = pl.ds(pl.multiple_of(part * HD, HD), HD)
         queries = q_vm[:, pl.ds(pl.multiple_of(c * HD, HD), HD)]
         row = table_vm[pl.ds(head * nheads + c, 1), :]
         levels = jnp.broadcast_to(row, (BLK, HD))
         high = [jnp.full((BLK, BLK), -jnp.inf, jnp.float32) for _ in range(2)]
         for j in range(REACH):
-            keys = kv_own[0, c] if j == 0 else kv_in[j - 1, 0, c]
+            keys = kv_own[0, piece, :, columns] if j == 0 else kv_in[j - 1, 0, piece, :, columns]
             raw = lax.dot_general(
                 queries, keys, (((1,), (1,)), ((), ())), preferred_element_type=jnp.float32
             )
@@ -209,7 +228,7 @@
         mixed = jnp.zeros((2 * BLK, 2 * HD), jnp.float32)
         ones = jnp.ones((2 * BLK, HD), jnp.bfloat16)
         for j in range(REACH):
-            vals = kv_own[1, c] if j == 0 else kv_in[j - 1, 1, c]
+            vals = kv_own[1, piece, :, columns] if j == 0 else kv_in[j - 1, 1, piece, :, columns]
             weights = jnp.exp(scores_vm[:, pl.ds(j * 2 * BLK, 2 * BLK)] - top)
             mixed = mixed + jnp.dot(
                 weights.astype(jnp.bfloat16),
@@ -227,17 +246,22 @@
             out_sem.at[c],
         )
 
-    lax.fori_loop(0, nheads, one_head, 0)
+    lax.fori_loop(0, pieces, one_piece, 0)
+
+    def finish_out(c, carry):
+        out_copy(c).wait()
+        return carry
+
+    lax.fori_loop(0, nheads, finish_out, 0)
 
     def finish(c, carry):
-        out_copy(c).wait()
         for pair in range(2):
             kv_copy(0, pair, c, next_chip).wait_send()
             kv_copy(1, pair, c, partner).wait_send()
             kv_copy(2, pair, c, third_to).wait_send()
         return carry
 
-    lax.fori_loop(0, nheads, finish, 0)
+    lax.fori_loop(0, pieces, finish, 0)
     for which in range(2):
         tile_copy(which, head, 1, head_two).wait_send()
         tile_copy(which, head, 0, head_near).wait_send()
@@ -252,6 +276,7 @@
 def body(query, key, value, blocks, counts, buckets, edge, table):
     rows, width = query.shape
     nheads = width // HD
+    pieces = nheads // PIECE
     nctx = lax.axis_size("ctx")
     anywhere = pl.BlockSpec(memory_space=pl.ANY)
     scalars = pl.BlockSpec(memory_space=pltpu.SMEM)
@@ -263,24 +288,25 @@
     return pl.pallas_call(
         kernel,
         out_shape=jax.ShapeDtypeStruct((rows, width), jnp.bfloat16),
-        in_specs=[scalars, scalars] + [anywhere] * 5 + [pl.BlockSpec(memory_space=pltpu.VMEM)],
+        in_specs=[scalars, scalars] + [anywhere] * 6,
         out_specs=anywhere,
         scratch_shapes=[
             pltpu.VMEM((rows, width), jnp.bfloat16),
-            pltpu.VMEM((2, nheads, rows, HD), jnp.bfloat16),
-            pltpu.VMEM((3, 2, nheads, rows, HD), jnp.bfloat16),
+            pltpu.VMEM((2, pieces, rows, PIECE * HD), jnp.bfloat16),
+            pltpu.VMEM((3, 2, pieces, rows, PIECE * HD), jnp.bfloat16),
             pltpu.VMEM(tiles, jnp.int32),
             pltpu.VMEM((4,) + tiles, jnp.bfloat16),
             pltpu.VMEM((4,) + tiles, jnp.bfloat16),
             pltpu.VMEM((2, 8, BLK, BLK), jnp.int32),
             pltpu.VMEM((2, 8, BLK, BLK), jnp.float32),
+            pltpu.VMEM(table.shape, jnp.float32),
             pltpu.VMEM((table.shape[0], 128), jnp.float32),
             pltpu.VMEM((rows, 8 * BLK), jnp.float32),
             pltpu.VMEM((nheads, rows, HD), jnp.bfloat16),
-            pltpu.SemaphoreType.DMA((3 + 2 * nheads,)),
+            pltpu.SemaphoreType.DMA((4 + 2 * pieces,)),
             pltpu.SemaphoreType.DMA((nheads,)),
-            pltpu.SemaphoreType.DMA((3, 2, nheads)),
-            pltpu.SemaphoreType.DMA((3, 2, nheads)),
+            pltpu.SemaphoreType.DMA((3, 2, pieces)),
+            pltpu.SemaphoreType.DMA((3, 2, pieces)),
             pltpu.SemaphoreType.DMA((2, 4)),
             pltpu.SemaphoreType.DMA((2, 4)),
         ],

time: 119 us -> 97.7 us (0.82)
  Pallas kernels: 114 us -> 93.8 us
    pallas_call x1, Pallas kernels: 114 us -> 93.8 us  [body(): pl.pallas_call(kernel, out_shape=jax.ShapeDtypeStruct((rows, width), jnp....]
where the time goes in v2:
time: 97.7 us; the launch traced here: 97.1 us
  Pallas kernels  93.8 us (96%)
  local copies, waits for them, and re-layouts  3.37 us (3%)
    pallas_call x1, Pallas kernels, body(): pl.pallas_call(kernel, out_shape=jax.ShapeDtypeStruct((rows, width), jnp....  93.8 us
    unnamed x2, local copies, waits for them, and re-layouts  3.37 us

profile of v2, /device:TPU:32, one launch (start us, length us, event | category | flops | bytes accessed | tf_op | source)
XLA Modules:
  0.0 97.1 jit_solution(9699286471582578645)
XLA Ops:
  0.0 1.4 %copy.9.refs_7_ = f32[40,32]{1,0:T(8,128)} copy(f32[40,32]{0,1:T(8,128)} %param.15) | data formatting | bytes 10240 | tf_op args[7]
  1.4 93.8 %attention.1 = bf16[256,1280]{1,0:T(8,128)(2,1)} custom-call(s32[2,8]{1,0:T(2,128)} %refs_0_.1, s32[2]{0:T(128)} %refs_1_.1, bf16[256,1280]{1,0:T(8,128)(2,1)} %refs_2_.1, bf16[256,1280]{1,0:T(8,128)(2,1)} %refs_3_.1, bf16[256,1280]{1,0:T(8,128)(2,1)} %refs_4_.1, s32[2,2,128,128]{3,2,1,0:T(8,128)} %refs_5_.1, bf16[2,2,128,128]{3,2,1,0:T(8,128)(2,1)} %refs_6_.1, ...), custom_call_target="tpu_custom_call" | custom-call | tf_op jit(solution)/shard_map/attention/pallas_call | solution.py:288
  95.2 2.0 %copy.11 = bf16[256,1280]{1,0:T(8,128)(2,1)} copy(bf16[256,1280]{1,0:T(8,128)(2,1)} %attention.1) | data formatting | bytes 1310720

commit v3 on v1

--- a/solution.py
+++ b/solution.py
@@ -9,6 +9,7 @@
 BLK = 128
 REACH = 4
 DEAD = -1e30
+AHEAD = 4
 MESH = pl.DeviceIdType.MESH
 
 
@@ -21,8 +22,8 @@
     v_hbm,
     buckets_hbm,
     edge_hbm,
-    table_ref,
-    out_hbm,
+    table_hbm,
+    out_ref,
     q_vm,
     kv_own,
     kv_in,
@@ -31,18 +32,17 @@
     edge_all,
     index_vm,
     edge_vm,
+    table_raw,
     table_vm,
     scores_vm,
-    out_vm,
     local_sem,
-    out_sem,
     kv_send,
     kv_recv,
     tile_send,
     tile_recv,
 ):
     nheads = kv_own.shape[1]
-    nlevels = table_ref.shape[1]
+    nlevels = table_raw.shape[0]
     ctx = lax.axis_index("ctx")
     head = lax.axis_index("head")
     core = lax.rem(ctx, 2)
@@ -61,16 +61,18 @@
     bucket_load = pltpu.make_async_copy(buckets_hbm, bucket_raw, local_sem.at[0])
     edge_load = pltpu.make_async_copy(edge_hbm, edge_all.at[head], local_sem.at[1])
     q_load = pltpu.make_async_copy(q_hbm, q_vm, local_sem.at[2])
+    table_load = pltpu.make_async_copy(table_hbm, table_raw, local_sem.at[3])
     bucket_load.start()
     edge_load.start()
     q_load.start()
+    table_load.start()
 
     def own_load(pair, c):
         src = (k_hbm, v_hbm)[pair]
         return pltpu.make_async_copy(
             src.at[:, pl.ds(pl.multiple_of(c * HD, HD), HD)],
             kv_own.at[pair, c],
-            local_sem.at[3 + pair * nheads + c],
+            local_sem.at[4 + pair * nheads + c],
         )
 
     def load_own(c, carry):
@@ -143,10 +145,12 @@
             kv_copy(2, pair, c, third_to).start()
         return carry
 
-    lax.fori_loop(0, nheads, send_own, 0)
-
+    lax.fori_loop(0, AHEAD, send_own, 0)
+
+    table_load.wait()
     table_vm[...] = jnp.full_like(table_vm, DEAD)
-    table_vm[:, 0:nlevels] = table_ref[...]
+    table_vm[0:nlevels, 0 : table_raw.shape[1]] = table_raw[...]
+    table_vm[...] = table_vm[...].T
 
     for which in range(2):
         tile_copy(which, head_two, 1, head_two).wait_recv()
@@ -178,17 +182,18 @@
     q_load.wait()
     scale = HD ** (-0.5)
 
-    def one_head(c, carry):
+    def arrive(c):
         for pair in range(2):
             kv_copy(0, pair, c, next_chip).wait_recv()
             kv_copy(1, pair, c, partner).start()
+
+    def attend(c):
         for pair in range(2):
             own_load(pair, c).wait()
             kv_copy(2, pair, c, third_to).wait_recv()
-        for pair in range(2):
             kv_copy(1, pair, c, partner).wait_recv()
-
-        queries = q_vm[:, pl.ds(pl.multiple_of(c * HD, HD), HD)]
+        columns = pl.ds(pl.multiple_of(c * HD, HD), HD)
+        queries = q_vm[:, columns]
         row = table_vm[pl.ds(head * nheads + c, 1), :]
         levels = jnp.broadcast_to(row, (BLK, HD))
         high = [jnp.full((BLK, BLK), -jnp.inf, jnp.float32) for _ in range(2)]
@@ -216,21 +221,26 @@
                 jnp.concatenate([vals, ones], axis=1),
                 preferred_element_type=jnp.float32,
             )
-        out_vm[c] = (mixed[:, :HD] / mixed[:, HD:]).astype(jnp.bfloat16)
-        out_copy(c).start()
+        out_ref[:, columns] = (mixed[:, :HD] / mixed[:, HD:]).astype(jnp.bfloat16)
+
+    def one_head(c, carry):
+        @pl.when(c < nheads)
+        def _():
+            arrive(c)
+
+        @pl.when(c + AHEAD < nheads)
+        def _():
+            send_own(c + AHEAD, 0)
+
+        @pl.when(c > 0)
+        def _():
+            attend(c - 1)
+
         return carry
 
-    def out_copy(c):
-        return pltpu.make_async_copy(
-            out_vm.at[c],
-            out_hbm.at[:, pl.ds(pl.multiple_of(c * HD, HD), HD)],
-            out_sem.at[c],
-        )
-
-    lax.fori_loop(0, nheads, one_head, 0)
+    lax.fori_loop(0, nheads + 1, one_head, 0)
 
     def finish(c, carry):
-        out_copy(c).wait()
         for pair in range(2):
             kv_copy(0, pair, c, next_chip).wait_send()
             kv_copy(1, pair, c, partner).wait_send()
@@ -262,9 +272,9 @@
 
     return pl.pallas_call(
         kernel,
-        out_shape=jax.ShapeDtypeStruct((rows, width), jnp.bfloat16),
-        in_specs=[scalars, scalars] + [anywhere] * 5 + [pl.BlockSpec(memory_space=pltpu.VMEM)],
-        out_specs=anywhere,
+        out_shape=pltpu.VMEM((rows, width), jnp.bfloat16),
+        in_specs=[scalars, scalars] + [anywhere] * 6,
+        out_specs=pl.BlockSpec(memory_space=pltpu.VMEM),
         scratch_shapes=[
             pltpu.VMEM((rows, width), jnp.bfloat16),
             pltpu.VMEM((2, nheads, rows, HD), jnp.bfloat16),
@@ -274,11 +284,10 @@
             pltpu.VMEM((4,) + tiles, jnp.bfloat16),
             pltpu.VMEM((2, 8, BLK, BLK), jnp.int32),
             pltpu.VMEM((2, 8, BLK, BLK), jnp.float32),
-            pltpu.VMEM((table.shape[0], 128), jnp.float32),
+            pltpu.VMEM(table.shape[::-1], jnp.float32),
+            pltpu.VMEM((128, 128), jnp.float32),
             pltpu.VMEM((rows, 8 * BLK), jnp.float32),
-            pltpu.VMEM((nheads, rows, HD), jnp.bfloat16),
-            pltpu.SemaphoreType.DMA((3 + 2 * nheads,)),
-            pltpu.SemaphoreType.DMA((nheads,)),
+            pltpu.SemaphoreType.DMA((4 + 2 * nheads,)),
             pltpu.SemaphoreType.DMA((3, 2, nheads)),
             pltpu.SemaphoreType.DMA((3, 2, nheads)),
             pltpu.SemaphoreType.DMA((2, 4)),
@@ -288,7 +297,7 @@
             collective_id=0, has_side_effects=True, vmem_limit_bytes=60 * 2**20
         ),
         name="attention",
-    )(blocks, counts, query, key, value, buckets, edge, table)
+    )(blocks, counts, query, key, value, buckets, edge, table.T)
 
 
 def solution(mesh):

time: 119 us -> 93.7 us (0.79); the launches traced: 117 us -> 93.6 us
  Pallas kernels: 114 us -> 92.8 us
  local copies, waits for them, and re-layouts: 3.37 us -> 0.84 us
    pallas_call x1, Pallas kernels: 114 us -> 92.8 us  [body(): pl.pallas_call(kernel, out_shape=pltpu.VMEM((rows, width), jnp.bfloat16),...]
    unnamed x2 -> x1, local copies, waits for them, and re-layouts: 3.37 us -> 0.84 us
where the time goes in v3:
time: 93.7 us; the launch traced here: 93.6 us
  Pallas kernels  92.8 us (99%)
    pallas_call x1, Pallas kernels, body(): pl.pallas_call(kernel, out_shape=pltpu.VMEM((rows, width), jnp.bfloat16),...  92.8 us

profile of v3, /device:TPU:32, one launch (start us, length us, event | category | flops | bytes accessed | tf_op | source)
XLA Modules:
  0.0 93.6 jit_solution(694322806863922208)
XLA Ops:
  0.0 92.8 %attention.1 = bf16[256,1280]{1,0:T(8,128)(2,1)S(1)} custom-call(s32[2,8]{1,0:T(2,128)} %refs_0_.1, s32[2]{0:T(128)} %refs_1_.1, bf16[256,1280]{1,0:T(8,128)(2,1)} %refs_2_.1, bf16[256,1280]{1,0:T(8,128)(2,1)} %refs_3_.1, bf16[256,1280]{1,0:T(8,128)(2,1)} %refs_4_.1, s32[2,2,128,128]{3,2,1,0:T(8,128)} %refs_5_.1, bf16[2,2,128,128]{3,2,1,0:T(8,128)(2,1)} %refs_6_.1, ...), custom_call_target="tpu_custom_call" | custom-call | tf_op jit(solution)/shard_map/attention/pallas_call | solution.py:273
  92.8 0.8 copy.10

commit v4 on v3

--- a/solution.py
+++ b/solution.py
@@ -10,6 +10,9 @@
 REACH = 4
 DEAD = -1e30
 AHEAD = 4
+LATE = 5
+TURNED = (9,)
+RELAY_AT = 3
 MESH = pl.DeviceIdType.MESH
 
 
@@ -40,6 +43,9 @@
     kv_recv,
     tile_send,
     tile_recv,
+    turn_in,
+    turn_send,
+    turn_recv,
 ):
     nheads = kv_own.shape[1]
     nlevels = table_raw.shape[0]
@@ -50,6 +56,9 @@
     head_two = lax.rem(head + 2, 4)
     head_far = 3 - head
     middle = jnp.logical_or(head == 1, head == 2)
+    upper = lax.rem(ctx, 4) // 2 == 1
+    turns = jnp.logical_and(jnp.logical_not(middle), upper)
+    relays = jnp.logical_and(jnp.logical_not(middle), jnp.logical_not(upper))
 
     def at_ctx(shift):
         return (lax.rem(ctx + shift + nctx, nctx), head)
@@ -57,6 +66,24 @@
     next_chip, prev_chip = at_ctx(2), at_ctx(-2)
     third_to, third_from = at_ctx(1 + 2 * core), at_ctx(2 * core - 3)
     partner = at_ctx(1 - 2 * core)
+
+    barrier = pltpu.get_barrier_semaphore()
+    peers = [
+        prev_chip,
+        third_from,
+        partner,
+        (ctx, head_near),
+        (ctx, head_two),
+        (ctx, head_far),
+    ]
+    for peer in peers:
+        pl.semaphore_signal(barrier, inc=1, device_id=peer, device_id_type=MESH)
+
+    @pl.when(relays)
+    def _():
+        pl.semaphore_signal(
+            barrier, inc=1, device_id=(prev_chip[0], head_far), device_id_type=MESH
+        )
 
     bucket_load = pltpu.make_async_copy(buckets_hbm, bucket_raw, local_sem.at[0])
     edge_load = pltpu.make_async_copy(edge_hbm, edge_all.at[head], local_sem.at[1])
@@ -79,22 +106,6 @@
         own_load(0, c).start()
         own_load(1, c).start()
         return carry
-
-    lax.fori_loop(0, nheads, load_own, 0)
-
-    barrier = pltpu.get_barrier_semaphore()
-    peers = [
-        next_chip,
-        prev_chip,
-        third_to,
-        third_from,
-        (ctx, head_near),
-        (ctx, head_two),
-        (ctx, head_far),
-    ]
-    for peer in peers:
-        pl.semaphore_signal(barrier, inc=1, device_id=peer, device_id_type=MESH)
-    pl.semaphore_wait(barrier, len(peers))
 
     def kv_copy(flow, pair, c, target):
         if flow == 1:
@@ -129,6 +140,7 @@
     bucket_load.wait()
     bucket_all[head] = bucket_raw[...].astype(jnp.float32).astype(jnp.bfloat16)
     edge_load.wait()
+    pl.semaphore_wait(barrier, len(peers) + jnp.where(turns, 1, 0))
     for which in range(2):
         tile_copy(which, head, 1, head_two).start()
         tile_copy(which, head, 0, head_near).start()
@@ -138,14 +150,50 @@
         for which in range(2):
             tile_copy(which, head, 2, head_far).start()
 
+    def turn_copy(pair, t):
+        return pltpu.make_async_remote_copy(
+            src_ref=(k_hbm, v_hbm)[pair].at[:, pl.ds(TURNED[t] * HD, HD)],
+            dst_ref=turn_in.at[pair, t],
+            send_sem=kv_send.at[0, pair, TURNED[t]],
+            recv_sem=turn_recv.at[pair, t],
+            device_id=(next_chip[0], head_far),
+            device_id_type=MESH,
+        )
+
+    def relay_copy(pair, t):
+        return pltpu.make_async_remote_copy(
+            src_ref=turn_in.at[pair, t],
+            dst_ref=kv_in.at[0, pair, TURNED[t]],
+            send_sem=turn_send.at[pair, t],
+            recv_sem=kv_recv.at[0, pair, TURNED[t]],
+            device_id=(ctx, head_far),
+            device_id_type=MESH,
+        )
+
     def send_own(c, carry):
-        for pair in range(2):
-            kv_copy(0, pair, c, next_chip).start()
+        turned = c < 0
+        for piece in TURNED:
+            turned = jnp.logical_or(turned, c == piece)
+        turned = jnp.logical_and(turned, turns)
+
+        @pl.when(jnp.logical_not(turned))
+        def _():
+            for pair in range(2):
+                kv_copy(0, pair, c, next_chip).start()
+
         for pair in range(2):
             kv_copy(2, pair, c, third_to).start()
         return carry
 
-    lax.fori_loop(0, AHEAD, send_own, 0)
+    lax.fori_loop(0, 2, send_own, 0)
+
+    @pl.when(turns)
+    def _():
+        for t in range(len(TURNED)):
+            for pair in range(2):
+                turn_copy(pair, t).start()
+
+    lax.fori_loop(0, nheads, load_own, 0)
 
     table_load.wait()
     table_vm[...] = jnp.full_like(table_vm, DEAD)
@@ -163,6 +211,8 @@
     for which in range(2):
         tile_copy(which, head_near, 0, head_near).wait_recv()
         tile_copy(which, head_far, 2, head_near).wait_recv()
+
+    lax.fori_loop(2, AHEAD, send_own, 0)
 
     behind = (0, 2, 1 + 2 * core, 3 - 2 * core)
     for g in range(2):
@@ -223,31 +273,52 @@
             )
         out_ref[:, columns] = (mixed[:, :HD] / mixed[:, HD:]).astype(jnp.bfloat16)
 
-    def one_head(c, carry):
-        @pl.when(c < nheads)
-        def _():
-            arrive(c)
-
-        @pl.when(c + AHEAD < nheads)
-        def _():
-            send_own(c + AHEAD, 0)
-
-        @pl.when(c > 0)
-        def _():
-            attend(c - 1)
-
-        return carry
-
-    lax.fori_loop(0, nheads + 1, one_head, 0)
-
-    def finish(c, carry):
+    def sent(c):
         for pair in range(2):
             kv_copy(0, pair, c, next_chip).wait_send()
             kv_copy(1, pair, c, partner).wait_send()
             kv_copy(2, pair, c, third_to).wait_send()
+
+    def one_head(c, carry):
+        for t in range(len(TURNED)):
+
+            @pl.when(jnp.logical_and(relays, c == RELAY_AT + t))
+            def _():
+                for pair in range(2):
+                    turn_copy(pair, t).wait_recv()
+                    relay_copy(pair, t).start()
+
+        @pl.when(c < nheads)
+        def _():
+            arrive(c)
+
+        @pl.when(c + AHEAD < nheads)
+        def _():
+            send_own(c + AHEAD, 0)
+
+        @pl.when(c > 0)
+        def _():
+            attend(c - 1)
+
+        @pl.when(c >= LATE)
+        def _():
+            sent(c - LATE)
+
         return carry
 
-    lax.fori_loop(0, nheads, finish, 0)
+    lax.fori_loop(0, nheads + 1, one_head, 0)
+
+    def finish(c, carry):
+        sent(c)
+        return carry
+
+    lax.fori_loop(nheads + 1 - LATE, nheads, finish, 0)
+    @pl.when(relays)
+    def _():
+        for t in range(len(TURNED)):
+            for pair in range(2):
+                relay_copy(pair, t).wait_send()
+
     for which in range(2):
         tile_copy(which, head, 1, head_two).wait_send()
         tile_copy(which, head, 0, head_near).wait_send()
@@ -292,6 +363,9 @@
             pltpu.SemaphoreType.DMA((3, 2, nheads)),
             pltpu.SemaphoreType.DMA((2, 4)),
             pltpu.SemaphoreType.DMA((2, 4)),
+            pltpu.VMEM((2, len(TURNED), rows, HD), jnp.bfloat16),
+            pltpu.SemaphoreType.DMA((2, len(TURNED))),
+            pltpu.SemaphoreType.DMA((2, len(TURNED))),
         ],
         compiler_params=pltpu.CompilerParams(
             collective_id=0, has_side_effects=True, vmem_limit_bytes=60 * 2**20

time: 93.7 us -> 91 us (0.971)
  Pallas kernels: 92.8 us -> 90 us
    pallas_call x1, Pallas kernels: 92.8 us -> 90 us  [body(): pl.pallas_call(kernel, out_shape=pltpu.VMEM((rows, width), jnp.bfloat16),...]
where the time goes in v4:
time: 91 us; the launch traced here: 90.9 us
  Pallas kernels  90 us (99%)
    pallas_call x1, Pallas kernels, body(): pl.pallas_call(kernel, out_shape=pltpu.VMEM((rows, width), jnp.bfloat16),...  90 us

profile of v4, /device:TPU:32, one launch (start us, length us, event | category | flops | bytes accessed | tf_op | source)
XLA Modules:
  0.0 90.9 jit_solution(8445757301602007019)
XLA Ops:
  0.0 90.0 %attention.1 = bf16[256,1280]{1,0:T(8,128)(2,1)S(1)} custom-call(s32[2,8]{1,0:T(2,128)} %refs_0_.1, s32[2]{0:T(128)} %refs_1_.1, bf16[256,1280]{1,0:T(8,128)(2,1)} %refs_2_.1, bf16[256,1280]{1,0:T(8,128)(2,1)} %refs_3_.1, bf16[256,1280]{1,0:T(8,128)(2,1)} %refs_4_.1, s32[2,2,128,128]{3,2,1,0:T(8,128)} %refs_5_.1, bf16[2,2,128,128]{3,2,1,0:T(8,128)(2,1)} %refs_6_.1, ...), custom_call_target="tpu_custom_call" | custom-call | tf_op jit(solution)/shard_map/attention/pallas_call | solution.py:344
  90.0 0.8 copy.10

commit v5 on v4

--- a/solution.py
+++ b/solution.py
@@ -38,6 +38,7 @@
     table_raw,
     table_vm,
     scores_vm,
+    high_vm,
     local_sem,
     kv_send,
     kv_recv,
@@ -237,30 +238,41 @@
             kv_copy(0, pair, c, next_chip).wait_recv()
             kv_copy(1, pair, c, partner).start()
 
-    def attend(c):
-        for pair in range(2):
-            own_load(pair, c).wait()
-            kv_copy(2, pair, c, third_to).wait_recv()
-            kv_copy(1, pair, c, partner).wait_recv()
+    def score(c, j, high):
         columns = pl.ds(pl.multiple_of(c * HD, HD), HD)
-        queries = q_vm[:, columns]
-        row = table_vm[pl.ds(head * nheads + c, 1), :]
-        levels = jnp.broadcast_to(row, (BLK, HD))
-        high = [jnp.full((BLK, BLK), -jnp.inf, jnp.float32) for _ in range(2)]
-        for j in range(REACH):
-            keys = kv_own[0, c] if j == 0 else kv_in[j - 1, 0, c]
-            raw = lax.dot_general(
-                queries, keys, (((1,), (1,)), ((), ())), preferred_element_type=jnp.float32
-            )
-            for g in range(2):
-                for b in range(2):
-                    looked = jnp.take_along_axis(levels, index_vm[g, j * 2 + b], axis=1)
-                    bias = (looked * edge_vm[g, j * 2 + b]).astype(jnp.bfloat16)
-                    tile = raw[g * BLK : (g + 1) * BLK, b * BLK : (b + 1) * BLK] * scale
-                    tile = tile + bias.astype(jnp.float32)
-                    high[g] = jnp.maximum(high[g], tile)
-                    scores_vm[pl.ds(g * BLK, BLK), pl.ds((j * 2 + b) * BLK, BLK)] = tile
+        keys = kv_own[0, c] if j == 0 else kv_in[j - 1, 0, c]
+        levels = jnp.broadcast_to(table_vm[pl.ds(head * nheads + c, 1), :], (BLK, HD))
+        raw = lax.dot_general(
+            q_vm[:, columns], keys, (((1,), (1,)), ((), ())), preferred_element_type=jnp.float32
+        )
+        for g in range(2):
+            for b in range(2):
+                looked = jnp.take_along_axis(levels, index_vm[g, j * 2 + b], axis=1)
+                bias = (looked * edge_vm[g, j * 2 + b]).astype(jnp.bfloat16)
+                tile = raw[g * BLK : (g + 1) * BLK, b * BLK : (b + 1) * BLK] * scale
+                tile = tile + bias.astype(jnp.float32)
+                high[g] = tile if high[g] is None else jnp.maximum(high[g], tile)
+                scores_vm[pl.ds(g * BLK, BLK), pl.ds((j * 2 + b) * BLK, BLK)] = tile
+
+    def early(c):
+        own_load(0, c).wait()
+        high = [None, None]
+        score(c, 0, high)
+        score(c, 1, high)
+        kv_copy(2, 0, c, third_to).wait_recv()
+        score(c, 3, high)
+        for g in range(2):
+            high_vm[g] = high[g]
+
+    def late(c):
+        columns = pl.ds(pl.multiple_of(c * HD, HD), HD)
+        high = [high_vm[0], high_vm[1]]
+        kv_copy(1, 0, c, partner).wait_recv()
+        score(c, 2, high)
         top = jnp.concatenate([jnp.max(x, axis=1, keepdims=True) for x in high], axis=0)
+        own_load(1, c).wait()
+        kv_copy(2, 1, c, third_to).wait_recv()
+        kv_copy(1, 1, c, partner).wait_recv()
         mixed = jnp.zeros((2 * BLK, 2 * HD), jnp.float32)
         ones = jnp.ones((2 * BLK, HD), jnp.bfloat16)
         for j in range(REACH):
@@ -279,6 +291,23 @@
             kv_copy(1, pair, c, partner).wait_send()
             kv_copy(2, pair, c, third_to).wait_send()
 
+    def sent_tiles():
+        @pl.when(relays)
+        def _():
+            for t in range(len(TURNED)):
+                for pair in range(2):
+                    relay_copy(pair, t).wait_send()
+
+        for which in range(2):
+            tile_copy(which, head, 1, head_two).wait_send()
+            tile_copy(which, head, 0, head_near).wait_send()
+
+        @pl.when(middle)
+        def _():
+            for which in range(2):
+                tile_copy(which, head, 2, head_far).wait_send()
+                tile_copy(which, head_two, 3, head_near).wait_send()
+
     def one_head(c, carry):
         for t in range(len(TURNED)):
 
@@ -298,11 +327,17 @@
 
         @pl.when(c > 0)
         def _():
-            attend(c - 1)
+            late(c - 1)
+
+        @pl.when(c < nheads)
+        def _():
+            early(c)
 
         @pl.when(c >= LATE)
         def _():
             sent(c - LATE)
+
+        pl.when(c == nheads - 2)(sent_tiles)
 
         return carry
 
@@ -313,21 +348,6 @@
         return carry
 
     lax.fori_loop(nheads + 1 - LATE, nheads, finish, 0)
-    @pl.when(relays)
-    def _():
-        for t in range(len(TURNED)):
-            for pair in range(2):
-                relay_copy(pair, t).wait_send()
-
-    for which in range(2):
-        tile_copy(which, head, 1, head_two).wait_send()
-        tile_copy(which, head, 0, head_near).wait_send()
-
-    @pl.when(middle)
-    def _():
-        for which in range(2):
-            tile_copy(which, head, 2, head_far).wait_send()
-            tile_copy(which, head_two, 3, head_near).wait_send()
 
 
 def body(query, key, value, blocks, counts, buckets, edge, table):
@@ -358,6 +378,7 @@
             pltpu.VMEM(table.shape[::-1], jnp.float32),
             pltpu.VMEM((128, 128), jnp.float32),
             pltpu.VMEM((rows, 8 * BLK), jnp.float32),
+            pltpu.VMEM((2, BLK, BLK), jnp.float32),
             pltpu.SemaphoreType.DMA((4 + 2 * nheads,)),
             pltpu.SemaphoreType.DMA((3, 2, nheads)),
             pltpu.SemaphoreType.DMA((3, 2, nheads)),

time: 91 us -> 90.2 us (level)
  no operation moved by 1% of the time
where the time goes in v5:
time: 90.2 us; the launch traced here: 90.1 us
  Pallas kernels  89.3 us (99%)
    pallas_call x1, Pallas kernels, body(): pl.pallas_call(kernel, out_shape=pltpu.VMEM((rows, width), jnp.bfloat16),...  89.3 us

profile of v5, /device:TPU:32, one launch (start us, length us, event | category | flops | bytes accessed | tf_op | source)
XLA Modules:
  0.0 90.1 jit_solution(8859842197725422107)
XLA Ops:
  0.0 89.3 %attention.1 = bf16[256,1280]{1,0:T(8,128)(2,1)S(1)} custom-call(s32[2,8]{1,0:T(2,128)} %refs_0_.1, s32[2]{0:T(128)} %refs_1_.1, bf16[256,1280]{1,0:T(8,128)(2,1)} %refs_2_.1, bf16[256,1280]{1,0:T(8,128)(2,1)} %refs_3_.1, bf16[256,1280]{1,0:T(8,128)(2,1)} %refs_4_.1, s32[2,2,128,128]{3,2,1,0:T(8,128)} %refs_5_.1, bf16[2,2,128,128]{3,2,1,0:T(8,128)(2,1)} %refs_6_.1, ...), custom_call_target="tpu_custom_call" | custom-call | tf_op jit(solution)/shard_map/attention/pallas_call | solution.py:364
  89.3 0.8 copy.10

commit v6 on v5

--- a/solution.py
+++ b/solution.py
@@ -9,10 +9,9 @@
 BLK = 128
 REACH = 4
 DEAD = -1e30
-AHEAD = 4
 LATE = 5
 TURNED = (9,)
-RELAY_AT = 3
+RELAY_AT = 1
 MESH = pl.DeviceIdType.MESH
 
 
@@ -57,9 +56,10 @@
     head_two = lax.rem(head + 2, 4)
     head_far = 3 - head
     middle = jnp.logical_or(head == 1, head == 2)
+    outer = jnp.logical_not(middle)
     upper = lax.rem(ctx, 4) // 2 == 1
-    turns = jnp.logical_and(jnp.logical_not(middle), upper)
-    relays = jnp.logical_and(jnp.logical_not(middle), jnp.logical_not(upper))
+    turns = jnp.logical_and(outer, upper)
+    relays = jnp.logical_and(outer, jnp.logical_not(upper))
 
     def at_ctx(shift):
         return (lax.rem(ctx + shift + nctx, nctx), head)
@@ -142,14 +142,18 @@
     bucket_all[head] = bucket_raw[...].astype(jnp.float32).astype(jnp.bfloat16)
     edge_load.wait()
     pl.semaphore_wait(barrier, len(peers) + jnp.where(turns, 1, 0))
-    for which in range(2):
-        tile_copy(which, head, 1, head_two).start()
-        tile_copy(which, head, 0, head_near).start()
+    @pl.when(outer)
+    def _():
+        for which in range(2):
+            tile_copy(which, head, 1, head_two).start()
 
     @pl.when(middle)
     def _():
         for which in range(2):
             tile_copy(which, head, 2, head_far).start()
+
+    for which in range(2):
+        tile_copy(which, head, 0, head_near).start()
 
     def turn_copy(pair, t):
         return pltpu.make_async_remote_copy(
@@ -186,7 +190,9 @@
             kv_copy(2, pair, c, third_to).start()
         return carry
 
-    lax.fori_loop(0, 2, send_own, 0)
+    early_sent = jnp.where(middle, 1, 4)
+    ahead = jnp.where(middle, 4, 6)
+    lax.fori_loop(0, early_sent, send_own, 0)
 
     @pl.when(turns)
     def _():
@@ -202,18 +208,23 @@
     table_vm[...] = table_vm[...].T
 
     for which in range(2):
-        tile_copy(which, head_two, 1, head_two).wait_recv()
-
-    @pl.when(middle)
-    def _():
-        for which in range(2):
+        tile_copy(which, head_two, 3, head_near).wait_recv()
+
+        @pl.when(middle)
+        def _():
             tile_copy(which, head_two, 3, head_near).start()
+
+    for which in range(2):
+        tile_copy(which, head_far, 1, head_near).wait_recv()
+
+        @pl.when(middle)
+        def _():
+            tile_copy(which, head_far, 1, head_near).start()
 
     for which in range(2):
         tile_copy(which, head_near, 0, head_near).wait_recv()
-        tile_copy(which, head_far, 2, head_near).wait_recv()
-
-    lax.fori_loop(2, AHEAD, send_own, 0)
+
+    lax.fori_loop(early_sent, ahead, send_own, 0)
 
     behind = (0, 2, 1 + 2 * core, 3 - 2 * core)
     for g in range(2):
@@ -299,13 +310,18 @@
                     relay_copy(pair, t).wait_send()
 
         for which in range(2):
-            tile_copy(which, head, 1, head_two).wait_send()
             tile_copy(which, head, 0, head_near).wait_send()
+
+        @pl.when(outer)
+        def _():
+            for which in range(2):
+                tile_copy(which, head, 1, head_two).wait_send()
 
         @pl.when(middle)
         def _():
             for which in range(2):
                 tile_copy(which, head, 2, head_far).wait_send()
+                tile_copy(which, head_far, 1, head_near).wait_send()
                 tile_copy(which, head_two, 3, head_near).wait_send()
 
     def one_head(c, carry):
@@ -321,9 +337,9 @@
         def _():
             arrive(c)
 
-        @pl.when(c + AHEAD < nheads)
-        def _():
-            send_own(c + AHEAD, 0)
+        @pl.when(c + ahead < nheads)
+        def _():
+            send_own(c + ahead, 0)
 
         @pl.when(c > 0)
         def _():

time: 90.2 us -> 90.3 us (level); the launches traced: 90.1 us -> 88.5 us
  Pallas kernels: 89.3 us -> 87.7 us
    pallas_call x1, Pallas kernels: 89.3 us -> 87.7 us  [body(): pl.pallas_call(kernel, out_shape=pltpu.VMEM((rows, width), jnp.bfloat16),...]
where the time goes in v6:
time: 90.3 us; the launch traced here: 88.5 us
  Pallas kernels  87.7 us (97%)
    pallas_call x1, Pallas kernels, body(): pl.pallas_call(kernel, out_shape=pltpu.VMEM((rows, width), jnp.bfloat16),...  87.7 us

profile of v6, /device:TPU:32, one launch (start us, length us, event | category | flops | bytes accessed | tf_op | source)
XLA Modules:
  0.0 88.5 jit_solution(10683893198858711752)
XLA Ops:
  0.0 87.7 %attention.1 = bf16[256,1280]{1,0:T(8,128)(2,1)S(1)} custom-call(s32[2,8]{1,0:T(2,128)} %refs_0_.1, s32[2]{0:T(128)} %refs_1_.1, bf16[256,1280]{1,0:T(8,128)(2,1)} %refs_2_.1, bf16[256,1280]{1,0:T(8,128)(2,1)} %refs_3_.1, bf16[256,1280]{1,0:T(8,128)(2,1)} %refs_4_.1, s32[2,2,128,128]{3,2,1,0:T(8,128)} %refs_5_.1, bf16[2,2,128,128]{3,2,1,0:T(8,128)(2,1)} %refs_6_.1, ...), custom_call_target="tpu_custom_call" | custom-call | tf_op jit(solution)/shard_map/attention/pallas_call | solution.py:380
  87.7 0.8 copy.10
